TPU v7x, 32 devices: a whole 2x2x4 slice. The times are simulated.
32 devices in a mesh: ctx: 16 (over z, x, core), head: 2 (over y).
Axes of the slice: x: 2, y: 2, z: 4, core: 2. Of those that a mesh axis runs over, the one named last changes fastest.
Arguments:
- block_order: int32 [32], replicated, may hold values from 0 to 31, as said below
- queries: bfloat16 [6144, 4096], P('ctx', 'head'), may hold values from -12 to 12
- key_head_matrix: bfloat16 [6144, 1024], P('ctx', 'head'), may hold values from -6 to 6
- value_head_matrix: bfloat16 [6144, 1024], P('ctx', 'head'), may hold values from -6 to 6
- out_weight: bfloat16 [4096, 4096], P('head'), may hold values from -0.125 to 0.125
- filter_taps: float32 [128, 4096], P(None, 'head'), may hold values from -0.5 to 0.5
- skip_gain: float32 [4096], P('head'), may hold values from 0.5 to 1.5
- gate_values: bfloat16 [6144, 4096], P('ctx', 'head'), may hold values from -4 to 4
Outputs:
- mixed_out: bfloat16 [6144, 4096], P('ctx', 'head')
Inputs may be any that keep to these rules, and one draw needn't show every extreme that they name: A permutation of the 32 sequence blocks; for every d, block_order[2 d] < 16 and block_order[2 d] + block_order[2 d + 1] = 31.
All inputs are finite; a program needn't handle non-finite values.
Results may differ from a plain program's by a relative error of at most 0.015.
Values may be sent and summed in bfloat16 or wider, within the bound.
A program may use at most 128 MiB of HBM per device.

v0:
```python
import math

import jax
import jax.numpy as jnp
from jax import lax
from jax.sharding import PartitionSpec as P

HEAD_WIDTH = 128
QUERY_PER_KV = 4


def lookup(table_values, index_values):
    matches = jnp.arange(table_values.shape[0], dtype=jnp.int32)[None, :] == index_values[:, None]
    return jnp.sum(jnp.where(matches, table_values[None, :], 0), axis=1)


def shards(
    block_order,
    queries,
    key_head_matrix,
    value_head_matrix,
    out_weight,
    filter_taps,
    skip_gain,
    gate_values,
):
    local_rows = queries.shape[0]
    block_rows = local_rows // 2
    shared_heads = key_head_matrix.shape[1] // HEAD_WIDTH
    position = lax.axis_index("ctx")
    own_blocks = 2 * position + jnp.arange(2, dtype=jnp.int32)
    own_order = lookup(block_order, own_blocks)
    query_place = (
        own_order[:, None] * block_rows + jnp.arange(block_rows, dtype=jnp.int32)[None, :]
    ).reshape(local_rows)
    query_heads = queries.reshape(local_rows, shared_heads, QUERY_PER_KV, HEAD_WIDTH)
    scaling = 1.0 / math.sqrt(HEAD_WIDTH)

    def attend_block(state_now, key_block, value_block, offset):
        running, row_total, summed = state_now
        key_count = key_block.shape[0]
        key_index = offset + jnp.arange(key_count, dtype=jnp.int32)
        key_place = (
            lookup(block_order, key_index // block_rows) * block_rows + key_index % block_rows
        )
        allowed = key_place[None, :] <= query_place[:, None]
        scores = (
            jnp.einsum("qhgd,khd->hgqk", query_heads, key_block, preferred_element_type=jnp.float32)
            * scaling
        )
        scores = jnp.where(allowed, scores, -1e30)
        newest = jnp.maximum(running, jnp.max(scores, axis=-1))
        weight = jnp.where(allowed, jnp.exp(scores - newest[..., None]), 0.0)
        factor = jnp.exp(running - newest)
        row_total = row_total * factor + jnp.sum(weight, axis=-1)
        summed = summed * factor[..., None] + jnp.einsum(
            "hgqk,khd->hgqd",
            weight.astype(jnp.bfloat16),
            value_block,
            preferred_element_type=jnp.float32,
        )
        return (newest, row_total, summed)

    start_state = (
        jnp.full((shared_heads, QUERY_PER_KV, local_rows), -1e30, jnp.float32),
        jnp.zeros((shared_heads, QUERY_PER_KV, local_rows), jnp.float32),
        jnp.zeros((shared_heads, QUERY_PER_KV, local_rows, HEAD_WIDTH), jnp.float32),
    )
    key_piece = lax.all_gather(key_head_matrix, "ctx", axis=0, tiled=True)
    value_piece = lax.all_gather(value_head_matrix, "ctx", axis=0, tiled=True)
    key_count = key_piece.shape[0]
    sub_rows = math.gcd(key_count, 1024)
    steps_count = key_count // sub_rows
    key_split = key_piece.reshape(steps_count, sub_rows, shared_heads, HEAD_WIDTH)
    value_split = value_piece.reshape(steps_count, sub_rows, shared_heads, HEAD_WIDTH)

    def one_step(carried, operands):
        key_block, value_block, block_number = operands
        return (attend_block(carried, key_block, value_block, block_number * sub_rows), None)

    result, unused = lax.scan(
        one_step, start_state, (key_split, value_split, jnp.arange(steps_count, dtype=jnp.int32))
    )
    running, row_total, summed = result
    attended = (
        jnp.transpose(summed / row_total[..., None], (2, 0, 1, 3))
        .reshape(local_rows, -1)
        .astype(jnp.bfloat16)
    )
    partials = jnp.dot(attended, out_weight, preferred_element_type=jnp.float32)
    projected = lax.psum_scatter(
        partials.astype(jnp.bfloat16), "head", scatter_dimension=1, tiled=True
    )
    channels = projected.shape[1]
    reach_rows = filter_taps.shape[0] - 1
    blocks_here = projected.reshape(2, block_rows, channels)
    tail_rows = blocks_here[:, block_rows - reach_rows :, :]
    wanted = own_order - 1
    piece = lax.all_gather(tail_rows, "ctx", axis=0, tiled=True)
    piece_count = piece.shape[0]
    held_blocks = lookup(block_order, jnp.arange(piece_count, dtype=jnp.int32))
    matches = (held_blocks[None, :] == wanted[:, None]).astype(jnp.bfloat16)
    halo_rows = jnp.einsum(
        "sn,nrc->src", matches, piece, preferred_element_type=jnp.float32
    ).astype(jnp.bfloat16)
    extended = jnp.concatenate([halo_rows, blocks_here], axis=1).astype(jnp.float32)
    reversed_taps = jnp.flip(filter_taps, 0)
    kernel = reversed_taps[:, None, :]
    filtered = lax.conv_general_dilated(
        extended,
        kernel,
        (1,),
        "VALID",
        dimension_numbers=("NHC", "HIO", "NHC"),
        feature_group_count=channels,
        precision=lax.Precision.HIGHEST,
    )
    gate_here = gate_values.reshape(2, block_rows, channels).astype(jnp.float32)
    mixed_rows = gate_here * (filtered + skip_gain[None, None, :] * blocks_here.astype(jnp.float32))
    return mixed_rows.reshape(local_rows, channels).astype(jnp.bfloat16)


def solution(mesh):
    return jax.shard_map(
        shards,
        mesh=mesh,
        in_specs=(
            P(),
            P("ctx", "head"),
            P("ctx", "head"),
            P("ctx", "head"),
            P("head", None),
            P(None, "head"),
            P("head"),
            P("ctx", "head"),
        ),
        out_specs=P("ctx", "head"),
        check_vma=False,
    )
```

profile of v0, /device:TPU:1, one launch (start us, length us, event | category | flops | bytes accessed | tf_op | source)
XLA Modules:
  0.0 640.6 jit_solution(9031850292084526371)
XLA Ops:
  6.5 0.7 all-gather.4.cloned.1.call-update
  7.3 0.7 all-gather.6.cloned.1.call-update
  8.1 1.9 copy.51
  10.0 1.0 copy.53
  11.2 0.6 broadcast_add_fusion
  11.7 62.3 %all-gather.4.cloned.1.call-done = bf16[6144,512]{1,0:T(8,128)(2,1)} async-done(((bf16[384,512]{1,0:T(8,128)(2,1)}), bf16[6144,512]{1,0:T(8,128)(2,1)}) %all-gather.4.cloned.1.call-update) | async-done | bytes 6291472 | tf_op jit(solution)/shard_map/all_gather | solution.py:69
  74.0 9.8 %reshape.67 = bf16[6,1024,4,128]{3,2,1,0:T(4,128)(2,1)} reshape(bf16[6144,512]{1,0:T(8,128)(2,1)} %all-gather.4.cloned.1.call-done) | data formatting | bytes 12582912 | tf_op jit(solution)/shard_map/reshape | solution.py:74
  83.8 53.0 %all-gather.6.cloned.1.call-done = bf16[6144,512]{1,0:T(8,128)(2,1)} async-done(((bf16[384,512]{1,0:T(8,128)(2,1)}), bf16[6144,512]{1,0:T(8,128)(2,1)}) %all-gather.6.cloned.1.call-update) | async-done | bytes 6291472 | tf_op jit(solution)/shard_map/all_gather | solution.py:70
  136.8 9.7 %reshape.69 = bf16[6,1024,4,128]{3,2,1,0:T(4,128)(2,1)} reshape(bf16[6144,512]{1,0:T(8,128)(2,1)} %all-gather.6.cloned.1.call-done) | data formatting | bytes 12582912 | tf_op jit(solution)/shard_map/reshape | solution.py:75
  146.5 241.7 %while.17 = (s32[]{:T(128)}, f32[4,4,384]{2,1,0:T(4,128)S(1)}, f32[4,4,384]{2,1,0:T(4,128)S(1)}, f32[4,4,384,128]{3,2,1,0:T(8,128)}, s32[6]{0:T(128)S(1)}, /*ind...) while((s32[]{:T(128)}, f32[4,4,384]{2,1,0:T(4,128)S(1)}, ...), condition=%wide.region_6.7_spmd.clone, body=%wide.region_2.6_spmd.clone.sunk | while | flops 3305913856 | bytes 116816232 | solution.py:81
  146.5 0.6 dynamic_slice.28
  147.9 0.3 broadcast_compare_fusion.2
  148.2 2.3 constant_dynamic-slice_fusion.3
  150.5 10.5 %fusion.46 = (f32[4,4,384]{2,1,0:T(4,128)S(1)}, f32[4,1024,384,4]{2,1,3,0:T(8,128)}) fusion(pred[384,1024]{0,1:T(8,128)(4,1)S(1)} %broadcast_compare_fusion.2, bf16[384,4,4,128]{3,0,2,1:T(8,128)(2,1)S(1)} %get-tuple-element.346, bf16[1,1024,4,128]{3,2,1,0:T(4,128)(2,1)S(1)} %get-tuple-element.307), kind=kOutput, calls=%fused_computation.3.clone.1 | convolution fusion | flops 1629480960 | bytes 28205056 | tf_op jit(solution)/shard_map/while/body/eval_jaxpr/qhgd,khd->hgqk/dot_general | solution.py:48
  161.1 11.6 %fusion.47 = f32[4,4,384]{2,1,0:T(4,128)S(1)} fusion(f32[4,1024,384,4]{2,1,3,0:T(8,128)} %get-tuple-element.309, f32[4,4,384]{2,1,0:T(4,128)S(1)} %select_maximum_fusion.2, pred[384,1024]{0,1:T(8,128)(4,1)S(1)} %broadcast_compare_fusion.2), kind=kLoop, calls=%fused_computation.5.clone.1 | loop fusion | flops 31451136 | bytes 25608192 | tf_op jit(solution)/shard_map/while/body/eval_jaxpr/reduce_sum | solution.py:55
  172.7 12.4 %fusion.49 = f32[4,4,384,128]{3,2,1,0:T(8,128)S(1)} fusion(f32[4,4,384,128]{3,2,1,0:T(8,128)S(1)} %copy-done.1, f32[4,1024,384,4]{2,1,3,0:T(8,128)} %get-tuple-element.309, f32[4,4,384]{2,1,0:T(4,128)S(1)} %select_maximum_fusion.2, pred[384,1024]{0,1:T(8,128)(4,1)S(1)} %broadcast_compare_fusion.2, f32[4,4,384]{2,1,0:T(4,128)S(1)} %get-tuple-element.311, ...), kind=kOutput, calls=%fused_computation.9.clone.1 | convolution fusion | flops 1644429312 | bytes 32948224 | tf_op jit(solution)/shard_map/while/body/eval_jaxpr/hgqk,khd->hgqd/dot_general | solution.py:56
  185.2 1.6 copy-done.2
  186.8 0.6 dynamic_slice.28
  188.2 0.3 broadcast_compare_fusion.2
  188.5 2.3 constant_dynamic-slice_fusion.3
  190.8 10.5 %fusion.46 = (f32[4,4,384]{2,1,0:T(4,128)S(1)}, f32[4,1024,384,4]{2,1,3,0:T(8,128)}) fusion(pred[384,1024]{0,1:T(8,128)(4,1)S(1)} %broadcast_compare_fusion.2, bf16[384,4,4,128]{3,0,2,1:T(8,128)(2,1)S(1)} %get-tuple-element.346, bf16[1,1024,4,128]{3,2,1,0:T(4,128)(2,1)S(1)} %get-tuple-element.307), kind=kOutput, calls=%fused_computation.3.clone.1 | convolution fusion | flops 1629480960 | bytes 28205056 | tf_op jit(solution)/shard_map/while/body/eval_jaxpr/qhgd,khd->hgqk/dot_general | solution.py:48
  201.3 11.6 %fusion.47 = f32[4,4,384]{2,1,0:T(4,128)S(1)} fusion(f32[4,1024,384,4]{2,1,3,0:T(8,128)} %get-tuple-element.309, f32[4,4,384]{2,1,0:T(4,128)S(1)} %select_maximum_fusion.2, pred[384,1024]{0,1:T(8,128)(4,1)S(1)} %broadcast_compare_fusion.2), kind=kLoop, calls=%fused_computation.5.clone.1 | loop fusion | flops 31451136 | bytes 25608192 | tf_op jit(solution)/shard_map/while/body/eval_jaxpr/reduce_sum | solution.py:55
  213.0 12.4 %fusion.49 = f32[4,4,384,128]{3,2,1,0:T(8,128)S(1)} fusion(f32[4,4,384,128]{3,2,1,0:T(8,128)S(1)} %copy-done.1, f32[4,1024,384,4]{2,1,3,0:T(8,128)} %get-tuple-element.309, f32[4,4,384]{2,1,0:T(4,128)S(1)} %select_maximum_fusion.2, pred[384,1024]{0,1:T(8,128)(4,1)S(1)} %broadcast_compare_fusion.2, f32[4,4,384]{2,1,0:T(4,128)S(1)} %get-tuple-element.311, ...), kind=kOutput, calls=%fused_computation.9.clone.1 | convolution fusion | flops 1644429312 | bytes 32948224 | tf_op jit(solution)/shard_map/while/body/eval_jaxpr/hgqk,khd->hgqd/dot_general | solution.py:56
  225.5 1.6 copy-done.2
  227.1 0.6 dynamic_slice.28
  228.8 2.3 constant_dynamic-slice_fusion.3
  231.1 10.5 %fusion.46 = (f32[4,4,384]{2,1,0:T(4,128)S(1)}, f32[4,1024,384,4]{2,1,3,0:T(8,128)}) fusion(pred[384,1024]{0,1:T(8,128)(4,1)S(1)} %broadcast_compare_fusion.2, bf16[384,4,4,128]{3,0,2,1:T(8,128)(2,1)S(1)} %get-tuple-element.346, bf16[1,1024,4,128]{3,2,1,0:T(4,128)(2,1)S(1)} %get-tuple-element.307), kind=kOutput, calls=%fused_computation.3.clone.1 | convolution fusion | flops 1629480960 | bytes 28205056 | tf_op jit(solution)/shard_map/while/body/eval_jaxpr/qhgd,khd->hgqk/dot_general | solution.py:48
  241.6 11.6 %fusion.47 = f32[4,4,384]{2,1,0:T(4,128)S(1)} fusion(f32[4,1024,384,4]{2,1,3,0:T(8,128)} %get-tuple-element.309, f32[4,4,384]{2,1,0:T(4,128)S(1)} %select_maximum_fusion.2, pred[384,1024]{0,1:T(8,128)(4,1)S(1)} %broadcast_compare_fusion.2), kind=kLoop, calls=%fused_computation.5.clone.1 | loop fusion | flops 31451136 | bytes 25608192 | tf_op jit(solution)/shard_map/while/body/eval_jaxpr/reduce_sum | solution.py:55
  253.3 12.4 %fusion.49 = f32[4,4,384,128]{3,2,1,0:T(8,128)S(1)} fusion(f32[4,4,384,128]{3,2,1,0:T(8,128)S(1)} %copy-done.1, f32[4,1024,384,4]{2,1,3,0:T(8,128)} %get-tuple-element.309, f32[4,4,384]{2,1,0:T(4,128)S(1)} %select_maximum_fusion.2, pred[384,1024]{0,1:T(8,128)(4,1)S(1)} %broadcast_compare_fusion.2, f32[4,4,384]{2,1,0:T(4,128)S(1)} %get-tuple-element.311, ...), kind=kOutput, calls=%fused_computation.9.clone.1 | convolution fusion | flops 1644429312 | bytes 32948224 | tf_op jit(solution)/shard_map/while/body/eval_jaxpr/hgqk,khd->hgqd/dot_general | solution.py:56
  265.8 1.6 copy-done.2
  267.4 0.6 dynamic_slice.28
  268.8 0.3 broadcast_compare_fusion.2
  269.1 2.3 constant_dynamic-slice_fusion.3
  271.4 10.5 %fusion.46 = (f32[4,4,384]{2,1,0:T(4,128)S(1)}, f32[4,1024,384,4]{2,1,3,0:T(8,128)}) fusion(pred[384,1024]{0,1:T(8,128)(4,1)S(1)} %broadcast_compare_fusion.2, bf16[384,4,4,128]{3,0,2,1:T(8,128)(2,1)S(1)} %get-tuple-element.346, bf16[1,1024,4,128]{3,2,1,0:T(4,128)(2,1)S(1)} %get-tuple-element.307), kind=kOutput, calls=%fused_computation.3.clone.1 | convolution fusion | flops 1629480960 | bytes 28205056 | tf_op jit(solution)/shard_map/while/body/eval_jaxpr/qhgd,khd->hgqk/dot_general | solution.py:48
  281.9 11.6 %fusion.47 = f32[4,4,384]{2,1,0:T(4,128)S(1)} fusion(f32[4,1024,384,4]{2,1,3,0:T(8,128)} %get-tuple-element.309, f32[4,4,384]{2,1,0:T(4,128)S(1)} %select_maximum_fusion.2, pred[384,1024]{0,1:T(8,128)(4,1)S(1)} %broadcast_compare_fusion.2), kind=kLoop, calls=%fused_computation.5.clone.1 | loop fusion | flops 31451136 | bytes 25608192 | tf_op jit(solution)/shard_map/while/body/eval_jaxpr/reduce_sum | solution.py:55
  293.6 12.4 %fusion.49 = f32[4,4,384,128]{3,2,1,0:T(8,128)S(1)} fusion(f32[4,4,384,128]{3,2,1,0:T(8,128)S(1)} %copy-done.1, f32[4,1024,384,4]{2,1,3,0:T(8,128)} %get-tuple-element.309, f32[4,4,384]{2,1,0:T(4,128)S(1)} %select_maximum_fusion.2, pred[384,1024]{0,1:T(8,128)(4,1)S(1)} %broadcast_compare_fusion.2, f32[4,4,384]{2,1,0:T(4,128)S(1)} %get-tuple-element.311, ...), kind=kOutput, calls=%fused_computation.9.clone.1 | convolution fusion | flops 1644429312 | bytes 32948224 | tf_op jit(solution)/shard_map/while/body/eval_jaxpr/hgqk,khd->hgqd/dot_general | solution.py:56
  306.1 1.6 copy-done.2
  307.7 0.6 dynamic_slice.28
  309.1 0.3 broadcast_compare_fusion.2
  309.4 2.3 constant_dynamic-slice_fusion.3
  311.7 10.5 %fusion.46 = (f32[4,4,384]{2,1,0:T(4,128)S(1)}, f32[4,1024,384,4]{2,1,3,0:T(8,128)}) fusion(pred[384,1024]{0,1:T(8,128)(4,1)S(1)} %broadcast_compare_fusion.2, bf16[384,4,4,128]{3,0,2,1:T(8,128)(2,1)S(1)} %get-tuple-element.346, bf16[1,1024,4,128]{3,2,1,0:T(4,128)(2,1)S(1)} %get-tuple-element.307), kind=kOutput, calls=%fused_computation.3.clone.1 | convolution fusion | flops 1629480960 | bytes 28205056 | tf_op jit(solution)/shard_map/while/body/eval_jaxpr/qhgd,khd->hgqk/dot_general | solution.py:48
  322.2 11.6 %fusion.47 = f32[4,4,384]{2,1,0:T(4,128)S(1)} fusion(f32[4,1024,384,4]{2,1,3,0:T(8,128)} %get-tuple-element.309, f32[4,4,384]{2,1,0:T(4,128)S(1)} %select_maximum_fusion.2, pred[384,1024]{0,1:T(8,128)(4,1)S(1)} %broadcast_compare_fusion.2), kind=kLoop, calls=%fused_computation.5.clone.1 | loop fusion | flops 31451136 | bytes 25608192 | tf_op jit(solution)/shard_map/while/body/eval_jaxpr/reduce_sum | solution.py:55
  333.9 12.4 %fusion.49 = f32[4,4,384,128]{3,2,1,0:T(8,128)S(1)} fusion(f32[4,4,384,128]{3,2,1,0:T(8,128)S(1)} %copy-done.1, f32[4,1024,384,4]{2,1,3,0:T(8,128)} %get-tuple-element.309, f32[4,4,384]{2,1,0:T(4,128)S(1)} %select_maximum_fusion.2, pred[384,1024]{0,1:T(8,128)(4,1)S(1)} %broadcast_compare_fusion.2, f32[4,4,384]{2,1,0:T(4,128)S(1)} %get-tuple-element.311, ...), kind=kOutput, calls=%fused_computation.9.clone.1 | convolution fusion | flops 1644429312 | bytes 32948224 | tf_op jit(solution)/shard_map/while/body/eval_jaxpr/hgqk,khd->hgqd/dot_general | solution.py:56
  346.4 1.6 copy-done.2
  348.0 0.6 dynamic_slice.28
  349.4 0.3 broadcast_compare_fusion.2
  349.7 2.3 constant_dynamic-slice_fusion.3
  352.0 10.5 %fusion.46 = (f32[4,4,384]{2,1,0:T(4,128)S(1)}, f32[4,1024,384,4]{2,1,3,0:T(8,128)}) fusion(pred[384,1024]{0,1:T(8,128)(4,1)S(1)} %broadcast_compare_fusion.2, bf16[384,4,4,128]{3,0,2,1:T(8,128)(2,1)S(1)} %get-tuple-element.346, bf16[1,1024,4,128]{3,2,1,0:T(4,128)(2,1)S(1)} %get-tuple-element.307), kind=kOutput, calls=%fused_computation.3.clone.1 | convolution fusion | flops 1629480960 | bytes 28205056 | tf_op jit(solution)/shard_map/while/body/eval_jaxpr/qhgd,khd->hgqk/dot_general | solution.py:48
  362.5 11.6 %fusion.47 = f32[4,4,384]{2,1,0:T(4,128)S(1)} fusion(f32[4,1024,384,4]{2,1,3,0:T(8,128)} %get-tuple-element.309, f32[4,4,384]{2,1,0:T(4,128)S(1)} %select_maximum_fusion.2, pred[384,1024]{0,1:T(8,128)(4,1)S(1)} %broadcast_compare_fusion.2), kind=kLoop, calls=%fused_computation.5.clone.1 | loop fusion | flops 31451136 | bytes 25608192 | tf_op jit(solution)/shard_map/while/body/eval_jaxpr/reduce_sum | solution.py:55
  374.2 12.4 %fusion.49 = f32[4,4,384,128]{3,2,1,0:T(8,128)S(1)} fusion(f32[4,4,384,128]{3,2,1,0:T(8,128)S(1)} %copy-done.1, f32[4,1024,384,4]{2,1,3,0:T(8,128)} %get-tuple-element.309, f32[4,4,384]{2,1,0:T(4,128)S(1)} %select_maximum_fusion.2, pred[384,1024]{0,1:T(8,128)(4,1)S(1)} %broadcast_compare_fusion.2, f32[4,4,384]{2,1,0:T(4,128)S(1)} %get-tuple-element.311, ...), kind=kOutput, calls=%fused_computation.9.clone.1 | convolution fusion | flops 1644429312 | bytes 32948224 | tf_op jit(solution)/shard_map/while/body/eval_jaxpr/hgqk,khd->hgqd/dot_general | solution.py:56
  386.6 1.6 copy-done.2
  388.3 2.4 copy.55
  390.6 0.3 divide_convert_fusion
  391.0 11.7 %convolution_convert_fusion = bf16[384,4096]{1,0:T(8,128)(2,1)} fusion(bf16[384,2048]{0,1:T(8,128)(2,1)S(1)} %bitcast.62, bf16[2048,4096]{1,0:T(8,128)(2,1)} %param.14), kind=kOutput, calls=%fused_computation.38 | convolution fusion | flops 6444023808 | bytes 21495808 | tf_op jit(solution)/shard_map/dot_general | solution.py:90
  402.7 41.6 %reduce-scatter.2.cloned.1.call-done = bf16[384,2048]{1,0:T(8,128)(2,1)} async-done(((bf16[384,4096]{1,0:T(8,128)(2,1)}), bf16[384,2048]{1,0:T(8,128)(2,1)}) %reduce-scatter.2.cloned.1.call-update) | async-done | bytes 1572880 | tf_op jit(solution)/shard_map/reduce_scatter | solution.py:91
  444.3 2.4 slice.4
  446.8 0.8 rev.4
  447.7 126.5 %all-gather.8.cloned.1.call-done = bf16[32,127,2048]{2,1,0:T(8,128)(2,1)} async-done(((bf16[2,127,2048]{2,1,0:T(8,128)(2,1)}), bf16[32,127,2048]{2,1,0:T(8,128)(2,1)}) %all-gather.8.cloned.1.call-update) | async-done | bytes 16646160 | tf_op jit(solution)/shard_map/all_gather | solution.py:99
  574.3 23.9 %fusion.22 = bf16[2,127,2048]{2,0,1:T(2,128)(2,1)S(1)} fusion(bf16[32,127,2048]{2,1,0:T(8,128)(2,1)} %all-gather.8.cloned.1.call-done, s32[32]{0:T(128)S(1)} %select_reduce_fusion.1, s32[2]{0:T(128)S(1)} %copy-done.7), kind=kOutput, calls=%fused_computation.36 | convolution fusion | flops 33292352 | bytes 17686664 | tf_op jit(solution)/shard_map/sn,nrc->src/dot_general | solution.py:103
  598.2 0.3 copy.80
  598.6 1.1 copy-done
  599.6 0.6 pad_maximum_fusion
  600.2 30.5 %fusion.25 = f32[2,192,2048]{2,0,1:T(2,128)S(1)} fusion(bf16[2,319,2048]{2,1,0:T(8,128)(2,1)S(1)} %pad_maximum_fusion, f32[128,1,2048]{2,0,1:T(8,128)S(1)} %bitcast.63), kind=kOutput, calls=%fused_computation.44 | convolution fusion | flops 1207959552 | bytes 6807552 | tf_op jit(solution)/shard_map/conv_general_dilated | solution.py:109
  630.7 3.2 fusion.24
  (91 shorter events, 2.8 us)
Async XLA Ops:
  6.5 67.5 %all-gather.4.cloned.1.call-start = ((), (), s32[]{:S(2)}) async-start(), calls=%async_computation.1 | async-start | bytes 6684672 | tf_op jit(solution)/shard_map/all_gather | solution.py:69
  7.3 129.5 %all-gather.6.cloned.1.call-start = ((), (), s32[]{:S(2)}) async-start(), calls=%async_computation.2 | async-start | bytes 6684672 | tf_op jit(solution)/shard_map/all_gather | solution.py:70
  8.0 436.3 %reduce-scatter.2.cloned.1.call-start = ((), (), s32[]{:S(2)}) async-start(), calls=%async_computation.3 | async-start | bytes 4718592 | tf_op jit(solution)/shard_map/reduce_scatter | solution.py:91
  8.1 2.9 copy-start.5
  161.0 11.7 %copy-start.1 = (f32[4,4,384,128]{3,2,1,0:T(8,128)S(1)}, f32[4,4,384,128]{3,2,1,0:T(8,128)}, u32[]{:S(2)}) copy-start(f32[4,4,384,128]{3,2,1,0:T(8,128)} %get-tuple-element.329) | copy-start | bytes 9437188 | tf_op jit(solution)/shard_map/while
  185.2 1.6 copy-start.2
  201.3 11.7 %copy-start.1 = (f32[4,4,384,128]{3,2,1,0:T(8,128)S(1)}, f32[4,4,384,128]{3,2,1,0:T(8,128)}, u32[]{:S(2)}) copy-start(f32[4,4,384,128]{3,2,1,0:T(8,128)} %get-tuple-element.329) | copy-start | bytes 9437188 | tf_op jit(solution)/shard_map/while
  225.5 1.6 copy-start.2
  241.6 11.7 %copy-start.1 = (f32[4,4,384,128]{3,2,1,0:T(8,128)S(1)}, f32[4,4,384,128]{3,2,1,0:T(8,128)}, u32[]{:S(2)}) copy-start(f32[4,4,384,128]{3,2,1,0:T(8,128)} %get-tuple-element.329) | copy-start | bytes 9437188 | tf_op jit(solution)/shard_map/while
  265.8 1.6 copy-start.2
  281.9 11.7 %copy-start.1 = (f32[4,4,384,128]{3,2,1,0:T(8,128)S(1)}, f32[4,4,384,128]{3,2,1,0:T(8,128)}, u32[]{:S(2)}) copy-start(f32[4,4,384,128]{3,2,1,0:T(8,128)} %get-tuple-element.329) | copy-start | bytes 9437188 | tf_op jit(solution)/shard_map/while
  306.0 1.6 copy-start.2
  322.2 11.7 %copy-start.1 = (f32[4,4,384,128]{3,2,1,0:T(8,128)S(1)}, f32[4,4,384,128]{3,2,1,0:T(8,128)}, u32[]{:S(2)}) copy-start(f32[4,4,384,128]{3,2,1,0:T(8,128)} %get-tuple-element.329) | copy-start | bytes 9437188 | tf_op jit(solution)/shard_map/while
  346.3 1.6 copy-start.2
  362.5 11.7 %copy-start.1 = (f32[4,4,384,128]{3,2,1,0:T(8,128)S(1)}, f32[4,4,384,128]{3,2,1,0:T(8,128)}, u32[]{:S(2)}) copy-start(f32[4,4,384,128]{3,2,1,0:T(8,128)} %get-tuple-element.329) | copy-start | bytes 9437188 | tf_op jit(solution)/shard_map/while
  386.6 1.6 copy-start.2
  402.6 44.2 %copy-start.4 = (f32[128,2048]{1,0:T(8,128)S(1)}, f32[128,2048]{1,0:T(8,128)}, u32[]{:S(2)}) copy-start(f32[128,2048]{1,0:T(8,128)} %param.15) | copy-start | bytes 3145732
  402.7 171.6 %copy-start.7 = (s32[2]{0:T(128)S(1)}, s32[2]{0:T(128)}, u32[]{:S(2)}) copy-start(s32[2]{0:T(128)} %get-tuple-element.238) | copy-start | bytes 28
  402.7 171.6 %all-gather.8.cloned.1.call-start = ((), (), s32[]{:S(2)}) async-start(), calls=%async_computation.4 | async-start | bytes 17825792 | tf_op jit(solution)/shard_map/all_gather | solution.py:99
  598.2 1.4 copy-start
  600.2 30.5 %copy-start.3 = (bf16[384,2048]{1,0:T(8,128)(2,1)S(1)}, bf16[384,2048]{1,0:T(8,128)(2,1)}, u32[]{:S(2)}) copy-start(bf16[384,2048]{1,0:T(8,128)(2,1)} %param.17) | copy-start | bytes 4718596
  600.2 30.5 %copy-start.6 = (f32[2048]{0:T(1024)S(1)}, f32[2048]{0:T(1024)}, u32[]{:S(2)}) copy-start(f32[2048]{0:T(1024)} %param.16) | copy-start | bytes 24580
Sparse Core Ops, SparseCore 0:
  9.6 64.3 all-gather.3
  76.3 60.4 all-gather.5
  402.8 41.5 reduce-scatter.1
  446.9 127.2 all-gather.7
where the time goes:
time: 651 us; the launch traced here: 641 us
  waiting for transfers between devices  285 us (44%)
  matrix products  204 us (31%)
  other arithmetic  77.7 us (12%)
  local copies, waits for them, and re-layouts  56.7 us (9%)
  between operations  13.5 us (2%)
    all_gather x1, waiting for transfers between devices, shards(): piece = lax.all_gather(tail_rows, 'ctx', axis=0, tiled=True)  127 us
    dot_general x6, matrix products, attend_block(): jnp.einsum('hgqk,khd->hgqd', weight.astype(jnp.bfloat16), value_block, pr...  74.7 us
    reduce_sum x6, other arithmetic, attend_block(): row_total = row_total * factor + jnp.sum(weight, axis=-1)  69.6 us
    dot_general x6, matrix products, attend_block(): jnp.einsum('qhgd,khd->hgqk', query_heads, key_block, preferred_element_ty...  63.3 us
    all_gather x1, waiting for transfers between devices, shards(): key_piece = lax.all_gather(key_head_matrix, 'ctx', axis=0, tiled=True)  62.3 us
    all_gather x1, waiting for transfers between devices, shards(): value_piece = lax.all_gather(value_head_matrix, 'ctx', axis=0, tiled=True)  53 us
    reduce_scatter x1, waiting for transfers between devices, shards(): lax.psum_scatter(partials.astype(jnp.bfloat16), 'head', scatter_dimension...  41.6 us
    conv_general_dilated x1, matrix products, shards(): lax.conv_general_dilated(extended, kernel, (1,), 'VALID', dimension_numbe...  30.5 us
  transfers between devices with their start and end apart: 4, of which 4 were waited for; matrix products, arithmetic and copies ran while one was open for 2% of the time, Pallas kernels for 0%

commit v1 on v0

v1 whole, which is shorter than its diff:
```python
import functools
import math

import jax
import jax.numpy as jnp
import ml_dtypes
import numpy as np
from jax import lax
from jax.experimental import pallas as pl
from jax.experimental.pallas import tpu as pltpu
from jax.sharding import PartitionSpec as P

HEAD_WIDTH = 128
QUERY_PER_KV = 4
VMEM_LIMIT = 56 * 1024 * 1024


def attention_kernel(order_ref, holder_ref, q_ref, k_ref, v_ref, out_ref, *, block_rows, devices, chunk):
    factor = math.log2(math.e) / math.sqrt(HEAD_WIDTH)
    rows = QUERY_PER_KV * block_rows

    def update(state, q, k, v, mask=None):
        top, acc = state
        s = lax.dot_general(q, k, (((1,), (1,)), ((), ())), preferred_element_type=jnp.float32) * factor
        if mask is not None:
            s = jnp.where(mask, s, -1e30)
        new_top = jnp.maximum(top, jnp.max(s, axis=1, keepdims=True))
        p = jnp.exp2(s - new_top)
        fade = jnp.exp2(top - new_top)
        v_ext = jnp.concatenate([v, jnp.ones_like(v)], axis=1)
        acc = acc * fade + jnp.dot(p.astype(jnp.bfloat16), v_ext, preferred_element_type=jnp.float32)
        return new_top, acc

    row_at = lax.broadcasted_iota(jnp.int32, (rows, block_rows), 0)
    row_at = lax.rem(row_at, block_rows)
    col_at = lax.broadcasted_iota(jnp.int32, (rows, block_rows), 1)
    diagonal = col_at <= row_at

    for half in range(2):
        q = jnp.concatenate(
            [
                q_ref[pl.ds(half * block_rows, block_rows), pl.ds(g * HEAD_WIDTH, HEAD_WIDTH)]
                for g in range(QUERY_PER_KV)
            ],
            axis=0,
        )
        own = holder_ref[order_ref[half]] // 2
        state = (
            jnp.full((rows, 1), -1e30, jnp.float32),
            jnp.zeros((rows, 2 * HEAD_WIDTH), jnp.float32),
        )
        state = update(state, q, k_ref[own, half], v_ref[own, half], diagonal)
        if half == 1:

            def low_step(i, state):
                k = k_ref[pl.ds(i * chunk, chunk), 0].reshape(chunk * block_rows, HEAD_WIDTH)
                v = v_ref[pl.ds(i * chunk, chunk), 0].reshape(chunk * block_rows, HEAD_WIDTH)
                return update(state, q, k, v)

            state = lax.fori_loop(0, devices // chunk, low_step, state)

        def step(j, state):
            at = holder_ref[j] // 2
            return update(state, q, k_ref[at, half], v_ref[at, half])

        state = lax.fori_loop(half * devices, order_ref[half], step, state)
        acc = state[1]
        result = (acc[:, :HEAD_WIDTH] / acc[:, HEAD_WIDTH:]).astype(jnp.bfloat16)
        for g in range(QUERY_PER_KV):
            out_ref[pl.ds(half * block_rows, block_rows), pl.ds(g * HEAD_WIDTH, HEAD_WIDTH)] = result[
                g * block_rows : (g + 1) * block_rows
            ]


def attention(own_order, holder, queries, keys, values, block_rows):
    local_rows, width = queries.shape
    devices = keys.shape[0]
    kv_heads = keys.shape[3] // HEAD_WIDTH
    group = QUERY_PER_KV * HEAD_WIDTH
    kv_spec = pl.BlockSpec((devices, 2, block_rows, HEAD_WIDTH), lambda h, *_: (0, 0, 0, h))
    return pl.pallas_call(
        functools.partial(
            attention_kernel, block_rows=block_rows, devices=devices, chunk=math.gcd(devices, 4)
        ),
        grid_spec=pltpu.PrefetchScalarGridSpec(
            num_scalar_prefetch=2,
            grid=(kv_heads,),
            in_specs=[pl.BlockSpec((local_rows, group), lambda h, *_: (0, h)), kv_spec, kv_spec],
            out_specs=pl.BlockSpec((local_rows, group), lambda h, *_: (0, h)),
        ),
        out_shape=jax.ShapeDtypeStruct((local_rows, width), jnp.bfloat16),
        compiler_params=pltpu.CompilerParams(vmem_limit_bytes=VMEM_LIMIT),
        name="attention",
    )(own_order, holder, queries, keys, values)


def split_bf16(array):
    high = array.astype(ml_dtypes.bfloat16)
    low = (array - high.astype(np.float64)).astype(ml_dtypes.bfloat16)
    return high, low


def transform_tables(taps, block_rows):
    size = taps + block_rows
    freq = np.arange(size // 2)[:, None] + 0.5
    angle = 2.0 * np.pi * freq * np.arange(size)[None, :] / size
    forward = np.concatenate([np.cos(angle), -np.sin(angle)], axis=0)
    back = np.concatenate([np.cos(angle), -np.sin(angle)], axis=0).T * (2.0 / size)
    back = back[taps:]
    fh, fl = split_bf16(forward)
    bh, bl = split_bf16(back)
    tap_table = np.concatenate([fh[:, :taps], fh[:, :taps], fl[:, :taps]], axis=1)
    signal_table = np.concatenate([fh, fl], axis=0)
    back_table = np.concatenate([bh, bh, bl], axis=1)
    return jnp.asarray(tap_table), jnp.asarray(signal_table), jnp.asarray(back_table)


def three_parts(x):
    high = x.astype(jnp.bfloat16)
    low = (x - high.astype(jnp.float32)).astype(jnp.bfloat16)
    return jnp.concatenate([high, low, high], axis=0)


def filter_kernel(tap_table, signal_table, back_table, taps_ref, skip_ref, halo_ref, x_ref, gate_ref, out_ref, *, block_rows):
    size = signal_table.shape[1]
    half_size = size // 2
    spectrum = jnp.dot(tap_table[...], three_parts(taps_ref[...]), preferred_element_type=jnp.float32)
    h_re, h_im = spectrum[:half_size], spectrum[half_size:]
    for block in range(2):
        rows = pl.ds(block * block_rows, block_rows)
        here = x_ref[rows, :]
        signal = jnp.concatenate([halo_ref[block], here], axis=0)
        both = jnp.dot(signal_table[...], signal, preferred_element_type=jnp.float32)
        both = both[:size] + both[size:]
        re, im = both[:half_size], both[half_size:]
        product = jnp.concatenate([re * h_re - im * h_im, re * h_im + im * h_re], axis=0)
        filtered = jnp.dot(back_table[...], three_parts(product), preferred_element_type=jnp.float32)
        mixed = gate_ref[rows, :].astype(jnp.float32) * (filtered + skip_ref[...] * here.astype(jnp.float32))
        out_ref[rows, :] = mixed.astype(jnp.bfloat16)


def causal_filter(projected, halo, filter_taps, skip_gain, gate_values, block_rows):
    local_rows, channels = projected.shape
    taps = filter_taps.shape[0]
    tables = transform_tables(taps, block_rows)
    tile = math.gcd(channels, 256)
    whole = [pl.BlockSpec(t.shape, lambda c: (0, 0)) for t in tables]
    rows_spec = pl.BlockSpec((local_rows, tile), lambda c: (0, c))
    return pl.pallas_call(
        functools.partial(filter_kernel, block_rows=block_rows),
        grid=(channels // tile,),
        in_specs=whole
        + [
            pl.BlockSpec((taps, tile), lambda c: (0, c)),
            pl.BlockSpec((1, tile), lambda c: (0, c)),
            pl.BlockSpec((2, taps, tile), lambda c: (0, 0, c)),
            rows_spec,
            rows_spec,
        ],
        out_specs=rows_spec,
        out_shape=jax.ShapeDtypeStruct((local_rows, channels), jnp.bfloat16),
        compiler_params=pltpu.CompilerParams(vmem_limit_bytes=VMEM_LIMIT),
        name="causal_filter",
    )(*tables, filter_taps, skip_gain[None, :], halo, projected, gate_values)


def shards(
    block_order,
    queries,
    key_head_matrix,
    value_head_matrix,
    out_weight,
    filter_taps,
    skip_gain,
    gate_values,
):
    local_rows = queries.shape[0]
    block_rows = local_rows // 2
    kv_width = key_head_matrix.shape[1]
    taps = filter_taps.shape[0]
    blocks = block_order.shape[0]
    devices = blocks // 2
    position = lax.axis_index("ctx")
    numbers = jnp.arange(blocks, dtype=jnp.int32)
    at_block = block_order[None, :] == numbers[:, None]
    holder = jnp.sum(jnp.where(at_block, numbers[None, :], 0), axis=1)
    own_order = lax.dynamic_slice(block_order, (2 * position,), (2,))

    keys = lax.all_gather(key_head_matrix, "ctx", axis=0, tiled=True)
    values = lax.all_gather(value_head_matrix, "ctx", axis=0, tiled=True)
    keys = keys.reshape(devices, 2, block_rows, kv_width)
    values = values.reshape(devices, 2, block_rows, kv_width)
    attended = attention(own_order, holder, queries, keys, values, block_rows)
    partials = jnp.dot(attended, out_weight, preferred_element_type=jnp.float32)
    projected = lax.psum_scatter(
        partials.astype(jnp.bfloat16), "head", scatter_dimension=1, tiled=True
    )
    channels = projected.shape[1]
    tails = projected.reshape(2, block_rows, channels)[:, block_rows - taps :, :]
    slices = lax.all_to_all(tails, "ctx", split_axis=1, concat_axis=0, tiled=True)
    wanted = (block_order[None, :] == block_order[:, None] - 1).astype(jnp.bfloat16)
    routed = jnp.dot(
        wanted, slices.reshape(blocks, -1), preferred_element_type=jnp.float32
    ).astype(jnp.bfloat16)
    routed = routed.reshape(slices.shape)
    halo = lax.all_to_all(routed, "ctx", split_axis=0, concat_axis=1, tiled=True)
    return causal_filter(projected, halo, filter_taps, skip_gain, gate_values, block_rows)


def solution(mesh):
    return jax.shard_map(
        shards,
        mesh=mesh,
        in_specs=(
            P(),
            P("ctx", "head"),
            P("ctx", "head"),
            P("ctx", "head"),
            P("head", None),
            P(None, "head"),
            P("head"),
            P("ctx", "head"),
        ),
        out_specs=P("ctx", "head"),
        check_vma=False,
    )
```

time: 651 us -> 353 us (0.54); the launches traced: 641 us -> 353 us
  matrix products: 204 us -> 12.3 us
  waiting for transfers between devices: 285 us -> 193 us
  Pallas kernels: 0 us -> 88.2 us
  other arithmetic: 77.7 us -> 1.31 us
  local copies, waits for them, and re-layouts: 56.7 us -> 7.34 us
  blocking collectives: 0 us -> 31.7 us
    dot_general x13 -> x1, matrix products: 162 us -> 0.47 us  [shards(): jnp.dot(wanted, slices.reshape(blocks, -1), preferred_element_type=jnp.fl...]
    all_gather x3 -> x2, waiting for transfers between devices: 242 us -> 126 us  [the longest x1 63.3 us: shards(): keys = lax.all_gather(key_head_matrix, 'ctx', axis=0, tiled=True)]
    pallas_call x0 -> x2, Pallas kernels: none -> 88.2 us  [the longest x1 76.3 us: attention(): pl.pallas_call(functools.partial(attention_kernel, block_rows=block_rows,...]
    reduce_sum x14 -> x1, other arithmetic: 70.5 us -> 1.31 us  [shards(): holder = jnp.sum(jnp.where(at_block, numbers[None, :], 0), axis=1)]
    all_to_all x0 -> x1, blocking collectives: none -> 31.7 us  [shards(): lax.all_to_all(routed, 'ctx', split_axis=0, concat_axis=1, tiled=True)]
    conv_general_dilated x1 -> x0, matrix products: 30.5 us -> none  [shards(): lax.conv_general_dilated(extended, kernel, (1,), 'VALID', dimension_numbe...]
    all_to_all x0 -> x1, waiting for transfers between devices: none -> 23.1 us  [shards(): lax.all_to_all(tails, 'ctx', split_axis=1, concat_axis=0, tiled=True)]
    reshape x2 -> x0, local copies, waits for them, and re-layouts: 19.5 us -> none  [the longest x1 9.75 us: shards(): key_piece.reshape(steps_count, sub_rows, shared_heads, HEAD_WIDTH)]
  transfers between devices with their start and end apart: 4 -> 4, of which waited for: 4 -> 4; matrix products, arithmetic and copies ran while one was open for 2% -> 1% of each run, Pallas kernels for 0% -> 0%
where the time goes in v1:
time: 353 us
  waiting for transfers between devices  193 us (55%)
  Pallas kernels  88.2 us (25%)
  blocking collectives  31.7 us (9%)
  between operations  13.2 us (4%)
  matrix products  12.3 us (3%)
  local copies, waits for them, and re-layouts  7.34 us (2%)
  starting transfers between devices  6.26 us (2%)
    pallas_call x1, Pallas kernels, attention(): pl.pallas_call(functools.partial(attention_kernel, block_rows=block_rows,...  76.3 us
    all_gather x1, waiting for transfers between devices, shards(): keys = lax.all_gather(key_head_matrix, 'ctx', axis=0, tiled=True)  63.3 us
    all_gather x1, waiting for transfers between devices, shards(): values = lax.all_gather(value_head_matrix, 'ctx', axis=0, tiled=True)  62.8 us
    reduce_scatter x1, waiting for transfers between devices, shards(): lax.psum_scatter(partials.astype(jnp.bfloat16), 'head', scatter_dimension...  41.9 us
    all_to_all x1, blocking collectives, shards(): lax.all_to_all(routed, 'ctx', split_axis=0, concat_axis=1, tiled=True)  31.7 us
    all_to_all x1, waiting for transfers between devices, shards(): lax.all_to_all(tails, 'ctx', split_axis=1, concat_axis=0, tiled=True)  23.1 us
    pallas_call x1, Pallas kernels, causal_filter(): pl.pallas_call(functools.partial(filter_kernel, block_rows=block_rows), g...  11.9 us
    dot_general x1, matrix products, shards(): partials = jnp.dot(attended, out_weight, preferred_element_type=jnp.float32)  11.8 us
  transfers between devices with their start and end apart: 4, of which 4 were waited for; matrix products, arithmetic and copies ran while one was open for 1% of the time, Pallas kernels for 0%

profile of v1, /device:TPU:1, one launch (start us, length us, event | category | flops | bytes accessed | tf_op | source)
XLA Modules:
  0.0 352.7 jit_solution(1606225646135119403)
XLA Ops:
  6.5 0.0 all-gather.3.cloned.1.call-start
  6.5 0.7 all-gather.3.cloned.1.call-update
  7.3 0.0 all-gather.5.cloned.1.call-start
  7.3 0.7 all-gather.5.cloned.1.call-update
  8.0 0.0 reduce-scatter.2.cloned.1.call-start
  8.1 1.3 dynamic_slice.3.order_ref
  9.4 1.3 select_reduce_fusion.holder_ref
  10.7 63.3 %all-gather.3.cloned.1.call-done = bf16[6144,512]{1,0:T(8,128)(2,1)} async-done(((bf16[384,512]{1,0:T(8,128)(2,1)}), bf16[6144,512]{1,0:T(8,128)(2,1)}) %all-gather.3.cloned.1.call-update) | async-done | bytes 6291472 | tf_op jit(solution)/shard_map/all_gather | solution.py:189
  74.0 62.8 %all-gather.5.cloned.1.call-done = bf16[6144,512]{1,0:T(8,128)(2,1)} async-done(((bf16[384,512]{1,0:T(8,128)(2,1)}), bf16[6144,512]{1,0:T(8,128)(2,1)}) %all-gather.5.cloned.1.call-update) | async-done | bytes 6291472 | tf_op jit(solution)/shard_map/all_gather | solution.py:190
  136.8 76.3 %attention.1 = bf16[384,2048]{1,0:T(8,128)(2,1)} custom-call(s32[2]{0:T(128)} %dynamic_slice.3.order_ref, s32[32]{0:T(128)} %select_reduce_fusion.holder_ref, bf16[384,2048]{1,0:T(8,128)(2,1)} %q_ref.1, bf16[16,2,192,512]{3,2,1,0:T(8,128)(2,1)} %bitcast.23, bf16[16,2,192,512]{3,2,1,0:T(8,128)(2,1)} %bitcast.24), custom_call_target="tpu_custom_call" | custom-call | tf_op jit(solution)/shard_map/attention/pallas_call | solution.py:81
  213.1 11.8 %convolution_convert_fusion.1 = bf16[384,4096]{1,0:T(8,128)(2,1)} fusion(bf16[384,2048]{1,0:T(8,128)(2,1)} %attention.1, bf16[2048,4096]{1,0:T(8,128)(2,1)} %param.15), kind=kOutput, calls=%fused_computation.1 | convolution fusion | flops 6444023808 | bytes 21495808 | tf_op jit(solution)/shard_map/dot_general | solution.py:194
  224.9 0.0 reduce-scatter.2.cloned.1.call-update
  225.0 41.9 %reduce-scatter.2.cloned.1.call-done.x_ref = bf16[384,2048]{1,0:T(8,128)(2,1)} async-done(((bf16[384,4096]{1,0:T(8,128)(2,1)}), bf16[384,2048]{1,0:T(8,128)(2,1)}) %reduce-scatter.2.cloned.1.call-update) | async-done | bytes 1572880 | tf_op jit(solution)/shard_map/reduce_scatter | solution.py:195
  266.8 0.0 copy-start
  266.8 1.3 slice.4
  268.1 2.0 copy.23
  270.2 6.2 %all-to-all-start = ((bf16[2,128,2048]{2,0,1:T(2,128)(2,1)}), bf16[2,128,2048]{2,0,1:T(2,128)(2,1)S(1)}, u32[]{:S(2)}, u32[]{:S(2)}) async-start(bf16[2,128,2048]{2,0,1:T(2,128)(2,1)} %copy.23), calls=%async_computation.1 | async-start | bytes 2097152 | tf_op jit(solution)/shard_map/all_to_all | solution.py:200
  276.4 0.0 copy-done
  276.4 23.1 %all-to-all-done = bf16[2,128,2048]{2,0,1:T(2,128)(2,1)S(1)} async-done(((bf16[2,128,2048]{2,0,1:T(2,128)(2,1)}), bf16[2,128,2048]{2,0,1:T(2,128)(2,1)S(1)}, u32[]{:S(2)}, u32[]{:S(2)}) %all-to-all-start) | async-done | bytes 1048608 | tf_op jit(solution)/shard_map/all_to_all | solution.py:200
  299.5 0.3 copy.29
  299.9 0.1 copy.21
  300.0 0.6 copy.24
  300.6 0.5 convolution_convert_fusion
  301.0 0.6 copy.25
  301.6 31.7 %all_to_all.33 = bf16[32,8,2048]{2,1,0:T(8,128)(2,1)S(1)} all-to-all(bf16[32,8,2048]{2,1,0:T(8,128)(2,1)S(1)} %bitcast.29), channel_id=1, replica_groups=mesh['ctx'=16,'head'=2] {'ctx'}, dimensions={0} | all-to-all | bytes 2097152 | tf_op jit(solution)/shard_map/all_to_all | solution.py:206
  333.3 1.0 copy.28
  334.3 11.9 %causal_filter.1 = bf16[384,2048]{1,0:T(8,128)(2,1)} custom-call(bf16[320,384]{1,0:T(8,128)(2,1)} %constant.21.clone.tap_table, bf16[640,320]{1,0:T(8,128)(2,1)} %constant.22.clone.signal_table, bf16[192,960]{1,0:T(8,128)(2,1)} %constant.23.clone.back_table, f32[128,2048]{1,0:T(8,128)} %taps_ref.1, f32[1,2048]{1,0:T(1,128)} %bitcast.33, ...), custom_call_target="tpu_custom_call" | custom-call | tf_op jit(solution)/shard_map/causal_filter/pallas_call | solution.py:149
  (1 shorter events, 0.0 us)
Async XLA Ops:
  6.5 67.5 %all-gather.3.cloned.1.call-start = ((), (), s32[]{:S(2)}) async-start(), calls=%async_computation.3 | async-start | bytes 6684672 | tf_op jit(solution)/shard_map/all_gather | solution.py:189
  7.3 129.5 %all-gather.5.cloned.1.call-start = ((), (), s32[]{:S(2)}) async-start(), calls=%async_computation.4 | async-start | bytes 6684672 | tf_op jit(solution)/shard_map/all_gather | solution.py:190
  8.0 258.8 %reduce-scatter.2.cloned.1.call-start = ((), (), s32[]{:S(2)}) async-start(), calls=%async_computation.5 | async-start | bytes 4718592 | tf_op jit(solution)/shard_map/reduce_scatter | solution.py:195
  266.8 9.5 %copy-start = (s32[32]{0:T(128)S(1)}, s32[32]{0:T(128)}, u32[]{:S(2)}) copy-start(s32[32]{0:T(128)} %param.11) | copy-start | bytes 388
  270.2 29.3 %all-to-all-start = ((bf16[2,128,2048]{2,0,1:T(2,128)(2,1)}), bf16[2,128,2048]{2,0,1:T(2,128)(2,1)S(1)}, u32[]{:S(2)}, u32[]{:S(2)}) async-start(bf16[2,128,2048]{2,0,1:T(2,128)(2,1)} %copy.23), calls=%async_computation.1 | async-start | bytes 2097152 | tf_op jit(solution)/shard_map/all_to_all | solution.py:200
Sparse Core Ops, SparseCore 0:
  9.6 64.3 all-gather.2
  76.3 60.4 all-gather.4
  225.1 41.6 reduce-scatter.1

commit v2 on v1

--- a/solution.py
+++ b/solution.py
@@ -72,26 +72,33 @@
             ]
 
 
-def attention(own_order, holder, queries, keys, values, block_rows):
-    local_rows, width = queries.shape
-    devices = keys.shape[0]
-    kv_heads = keys.shape[3] // HEAD_WIDTH
+def attention(own_order, holder, queries, pairs, head, block_rows):
+    local_rows = queries.shape[0]
+    devices = pairs.shape[0]
     group = QUERY_PER_KV * HEAD_WIDTH
-    kv_spec = pl.BlockSpec((devices, 2, block_rows, HEAD_WIDTH), lambda h, *_: (0, 0, 0, h))
+    pair_block = (devices, 2, block_rows, HEAD_WIDTH)
+    work = 2 * QUERY_PER_KV * block_rows * (devices + 1) * 2 * block_rows
     return pl.pallas_call(
         functools.partial(
             attention_kernel, block_rows=block_rows, devices=devices, chunk=math.gcd(devices, 4)
         ),
         grid_spec=pltpu.PrefetchScalarGridSpec(
             num_scalar_prefetch=2,
-            grid=(kv_heads,),
-            in_specs=[pl.BlockSpec((local_rows, group), lambda h, *_: (0, h)), kv_spec, kv_spec],
-            out_specs=pl.BlockSpec((local_rows, group), lambda h, *_: (0, h)),
-        ),
-        out_shape=jax.ShapeDtypeStruct((local_rows, width), jnp.bfloat16),
+            grid=(1,),
+            in_specs=[
+                pl.BlockSpec((local_rows, group), lambda i, *_: (0, head)),
+                pl.BlockSpec(pair_block, lambda i, *_: (0, 0, 0, 0)),
+                pl.BlockSpec(pair_block, lambda i, *_: (0, 0, 0, 1)),
+            ],
+            out_specs=pl.BlockSpec((local_rows, group), lambda i, *_: (0, 0)),
+        ),
+        out_shape=jax.ShapeDtypeStruct((local_rows, group), jnp.bfloat16),
         compiler_params=pltpu.CompilerParams(vmem_limit_bytes=VMEM_LIMIT),
+        cost_estimate=pl.CostEstimate(
+            flops=work * 4 * HEAD_WIDTH, bytes_accessed=2 * pairs.size, transcendentals=work
+        ),
         name="attention",
-    )(own_order, holder, queries, keys, values)
+    )(own_order, holder, queries, pairs, pairs)
 
 
 def split_bf16(array):
@@ -186,11 +193,19 @@
     holder = jnp.sum(jnp.where(at_block, numbers[None, :], 0), axis=1)
     own_order = lax.dynamic_slice(block_order, (2 * position,), (2,))
 
-    keys = lax.all_gather(key_head_matrix, "ctx", axis=0, tiled=True)
-    values = lax.all_gather(value_head_matrix, "ctx", axis=0, tiled=True)
-    keys = keys.reshape(devices, 2, block_rows, kv_width)
-    values = values.reshape(devices, 2, block_rows, kv_width)
-    attended = attention(own_order, holder, queries, keys, values, block_rows)
+    gathered = []
+    for head in range(kv_width // HEAD_WIDTH):
+        columns = slice(head * HEAD_WIDTH, (head + 1) * HEAD_WIDTH)
+        pair = jnp.concatenate([key_head_matrix[:, columns], value_head_matrix[:, columns]], axis=1)
+        pairs = lax.all_gather(pair, "ctx", axis=0, tiled=True)
+        gathered.append(pairs.reshape(devices, 2, block_rows, 2 * HEAD_WIDTH))
+    attended = jnp.concatenate(
+        [
+            attention(own_order, holder, queries, pairs, head, block_rows)
+            for head, pairs in enumerate(gathered)
+        ],
+        axis=1,
+    )
     partials = jnp.dot(attended, out_weight, preferred_element_type=jnp.float32)
     projected = lax.psum_scatter(
         partials.astype(jnp.bfloat16), "head", scatter_dimension=1, tiled=True

time: 353 us -> 358 us (1.014)
  Pallas kernels: 88.2 us -> 99.1 us
  waiting for transfers between devices: 193 us -> 184 us
    pallas_call x1 -> x4, Pallas kernels: 76.3 us -> 87.3 us  [attention(): pl.pallas_call(functools.partial(attention_kernel, block_rows=block_rows,...]
    all_gather x2 -> x4, waiting for transfers between devices: 126 us -> 119 us  [shards(): pairs = lax.all_gather(pair, 'ctx', axis=0, tiled=True)]
  transfers between devices with their start and end apart: 4 -> 6, of which waited for: 4 -> 6; matrix products, arithmetic and copies ran while one was open for 1% -> 1% of each run, Pallas kernels for 0% -> 18%
where the time goes in v2:
time: 358 us
  waiting for transfers between devices  184 us (51%)
  Pallas kernels  99.1 us (28%)
  blocking collectives  31.7 us (9%)
  between operations  13.2 us (4%)
  matrix products  12.1 us (3%)
  local copies, waits for them, and re-layouts  7.88 us (2%)
  starting transfers between devices  6.36 us (2%)
    all_gather x4, waiting for transfers between devices, shards(): pairs = lax.all_gather(pair, 'ctx', axis=0, tiled=True)  119 us
    pallas_call x4, Pallas kernels, attention(): pl.pallas_call(functools.partial(attention_kernel, block_rows=block_rows,...  87.3 us
    reduce_scatter x1, waiting for transfers between devices, shards(): lax.psum_scatter(partials.astype(jnp.bfloat16), 'head', scatter_dimension...  41.9 us
    all_to_all x1, blocking collectives, shards(): lax.all_to_all(routed, 'ctx', split_axis=0, concat_axis=1, tiled=True)  31.7 us
    all_to_all x1, waiting for transfers between devices, shards(): lax.all_to_all(tails, 'ctx', split_axis=1, concat_axis=0, tiled=True)  23.1 us
    pallas_call x1, Pallas kernels, causal_filter(): pl.pallas_call(functools.partial(filter_kernel, block_rows=block_rows), g...  11.9 us
    dot_general x1, matrix products, shards(): partials = jnp.dot(attended, out_weight, preferred_element_type=jnp.float32)  11.6 us
  transfers between devices with their start and end apart: 6, of which 6 were waited for; matrix products, arithmetic and copies ran while one was open for 1% of the time, Pallas kernels for 18%

profile of v2, /device:TPU:1, one launch (start us, length us, event | category | flops | bytes accessed | tf_op | source)
XLA Modules:
  0.0 357.8 jit_solution(6348230332738449789)
XLA Ops:
  6.5 0.0 copy-start
  6.5 0.0 all-gather.5.cloned.1.call-start
  6.5 1.3 fusion.11
  7.8 0.7 pad_maximum_fusion
  8.5 0.0 all-gather.5.cloned.1.call-update
  8.6 0.0 all-gather.7.cloned.1.call-start
  8.6 0.7 pad_maximum_fusion.1
  9.3 0.0 all-gather.7.cloned.1.call-update
  9.4 0.0 all-gather.9.cloned.1.call-start
  9.4 0.7 pad_maximum_fusion.2
  10.1 0.0 all-gather.9.cloned.1.call-update
  10.1 0.0 all-gather.11.cloned.1.call-start
  10.2 0.7 pad_maximum_fusion.3
  10.9 0.0 all-gather.11.cloned.1.call-update
  10.9 0.0 reduce-scatter.2.cloned.1.call-start
  11.0 0.0 copy-done
  11.0 0.6 dynamic_slice.3.order_ref
  11.5 0.6 select_reduce_fusion.holder_ref
  12.2 45.2 %all-gather.5.cloned.1.call-done = bf16[6144,256]{1,0:T(8,128)(2,1)} async-done(((bf16[384,256]{1,0:T(8,128)(2,1)}), bf16[6144,256]{1,0:T(8,128)(2,1)}) %all-gather.5.cloned.1.call-update) | async-done | bytes 3145744 | tf_op jit(solution)/shard_map/all_gather | solution.py:200
  57.4 21.8 %attention.4 = bf16[384,512]{1,0:T(8,128)(2,1)} custom-call(s32[2]{0:T(128)} %dynamic_slice.3.order_ref, s32[32]{0:T(128)} %select_reduce_fusion.holder_ref, bf16[384,2048]{1,0:T(8,128)(2,1)} %q_ref.7, bf16[16,2,192,256]{3,2,1,0:T(8,128)(2,1)} %bitcast.33, bf16[16,2,192,256]{3,2,1,0:T(8,128)(2,1)} %bitcast.34), custom_call_target="tpu_custom_call" | custom-call | flops 5133828096 | bytes 3145728 | tf_op jit(solution)/shard_map/attention/pallas_call | solution.py:81
  79.1 24.6 %all-gather.7.cloned.1.call-done = bf16[6144,256]{1,0:T(8,128)(2,1)} async-done(((bf16[384,256]{1,0:T(8,128)(2,1)}), bf16[6144,256]{1,0:T(8,128)(2,1)}) %all-gather.7.cloned.1.call-update) | async-done | bytes 3145744 | tf_op jit(solution)/shard_map/all_gather | solution.py:200
  103.7 21.7 %attention.5 = bf16[384,512]{1,0:T(8,128)(2,1)} custom-call(s32[2]{0:T(128)} %dynamic_slice.3.order_ref, s32[32]{0:T(128)} %select_reduce_fusion.holder_ref, bf16[384,2048]{1,0:T(8,128)(2,1)} %q_ref.7, bf16[16,2,192,256]{3,2,1,0:T(8,128)(2,1)} %bitcast.35, bf16[16,2,192,256]{3,2,1,0:T(8,128)(2,1)} %bitcast.36), custom_call_target="tpu_custom_call" | custom-call | flops 5133828096 | bytes 3145728 | tf_op jit(solution)/shard_map/attention/pallas_call | solution.py:81
  125.4 24.6 %all-gather.9.cloned.1.call-done = bf16[6144,256]{1,0:T(8,128)(2,1)} async-done(((bf16[384,256]{1,0:T(8,128)(2,1)}), bf16[6144,256]{1,0:T(8,128)(2,1)}) %all-gather.9.cloned.1.call-update) | async-done | bytes 3145744 | tf_op jit(solution)/shard_map/all_gather | solution.py:200
  150.0 21.9 %attention.6 = bf16[384,512]{1,0:T(8,128)(2,1)} custom-call(s32[2]{0:T(128)} %dynamic_slice.3.order_ref, s32[32]{0:T(128)} %select_reduce_fusion.holder_ref, bf16[384,2048]{1,0:T(8,128)(2,1)} %q_ref.7, bf16[16,2,192,256]{3,2,1,0:T(8,128)(2,1)} %bitcast.37, bf16[16,2,192,256]{3,2,1,0:T(8,128)(2,1)} %bitcast.38), custom_call_target="tpu_custom_call" | custom-call | flops 5133828096 | bytes 3145728 | tf_op jit(solution)/shard_map/attention/pallas_call | solution.py:81
  171.9 24.5 %all-gather.11.cloned.1.call-done = bf16[6144,256]{1,0:T(8,128)(2,1)} async-done(((bf16[384,256]{1,0:T(8,128)(2,1)}), bf16[6144,256]{1,0:T(8,128)(2,1)}) %all-gather.11.cloned.1.call-update) | async-done | bytes 3145744 | tf_op jit(solution)/shard_map/all_gather | solution.py:200
  196.4 0.0 copy-start.1
  196.4 0.0 copy-start.2
  196.4 0.0 copy-start.3
  196.4 21.9 %attention.7 = bf16[384,512]{1,0:T(8,128)(2,1)} custom-call(s32[2]{0:T(128)} %dynamic_slice.3.order_ref, s32[32]{0:T(128)} %select_reduce_fusion.holder_ref, bf16[384,2048]{1,0:T(8,128)(2,1)} %q_ref.7, bf16[16,2,192,256]{3,2,1,0:T(8,128)(2,1)} %bitcast.39, bf16[16,2,192,256]{3,2,1,0:T(8,128)(2,1)} %bitcast.40), custom_call_target="tpu_custom_call" | custom-call | flops 5133828096 | bytes 3145728 | tf_op jit(solution)/shard_map/attention/pallas_call | solution.py:81
  218.3 0.0 copy-done.1
  218.3 0.0 copy-done.2
  218.3 0.0 copy-done.3
  218.3 11.6 %convolution_convert_fusion.1 = bf16[384,4096]{1,0:T(8,128)(2,1)} fusion(bf16[2048,4096]{1,0:T(8,128)(2,1)} %param.15, bf16[384,512]{1,0:T(8,128)(2,1)} %attention.7, bf16[384,512]{1,0:T(8,128)(2,1)S(1)} %copy-done.3, bf16[384,512]{1,0:T(8,128)(2,1)S(1)} %copy-done.2, bf16[384,512]{1,0:T(8,128)(2,1)S(1)} %copy-done.1), kind=kOutput, calls=%fused_computation.1 | convolution fusion | flops 6450315264 | bytes 21495808 | tf_op jit(solution)/shard_map/dot_general | solution.py:209
  229.9 0.0 reduce-scatter.2.cloned.1.call-update
  229.9 41.9 %reduce-scatter.2.cloned.1.call-done.x_ref = bf16[384,2048]{1,0:T(8,128)(2,1)} async-done(((bf16[384,4096]{1,0:T(8,128)(2,1)}), bf16[384,2048]{1,0:T(8,128)(2,1)}) %reduce-scatter.2.cloned.1.call-update) | async-done | bytes 1572880 | tf_op jit(solution)/shard_map/reduce_scatter | solution.py:210
  271.8 1.3 slice.36
  273.1 2.0 copy.23
  275.2 6.2 %all-to-all-start = ((bf16[2,128,2048]{2,0,1:T(2,128)(2,1)}), bf16[2,128,2048]{2,0,1:T(2,128)(2,1)S(1)}, u32[]{:S(2)}, u32[]{:S(2)}) async-start(bf16[2,128,2048]{2,0,1:T(2,128)(2,1)} %copy.23), calls=%async_computation.1 | async-start | bytes 2097152 | tf_op jit(solution)/shard_map/all_to_all | solution.py:215
  281.4 23.1 %all-to-all-done = bf16[2,128,2048]{2,0,1:T(2,128)(2,1)S(1)} async-done(((bf16[2,128,2048]{2,0,1:T(2,128)(2,1)}), bf16[2,128,2048]{2,0,1:T(2,128)(2,1)S(1)}, u32[]{:S(2)}, u32[]{:S(2)}) %all-to-all-start) | async-done | bytes 1048608 | tf_op jit(solution)/shard_map/all_to_all | solution.py:215
  304.5 0.3 copy.29
  304.9 0.1 copy.21
  305.0 0.6 copy.24
  305.6 0.5 convolution_convert_fusion
  306.1 0.6 copy.25
  306.7 31.7 %all_to_all.33 = bf16[32,8,2048]{2,1,0:T(8,128)(2,1)S(1)} all-to-all(bf16[32,8,2048]{2,1,0:T(8,128)(2,1)S(1)} %bitcast.28), channel_id=1, replica_groups=mesh['ctx'=16,'head'=2] {'ctx'}, dimensions={0} | all-to-all | bytes 2097152 | tf_op jit(solution)/shard_map/all_to_all | solution.py:221
  338.3 1.0 copy.28
  339.4 11.9 %causal_filter.1 = bf16[384,2048]{1,0:T(8,128)(2,1)} custom-call(bf16[320,384]{1,0:T(8,128)(2,1)} %constant.21.clone.tap_table, bf16[640,320]{1,0:T(8,128)(2,1)} %constant.22.clone.signal_table, bf16[192,960]{1,0:T(8,128)(2,1)} %constant.23.clone.back_table, f32[128,2048]{1,0:T(8,128)} %taps_ref.1, f32[1,2048]{1,0:T(1,128)} %bitcast.32, ...), custom_call_target="tpu_custom_call" | custom-call | tf_op jit(solution)/shard_map/causal_filter/pallas_call | solution.py:156
  (1 shorter events, 0.0 us)
Async XLA Ops:
  6.5 4.4 %copy-start = (s32[32]{0:T(128)S(1)}, s32[32]{0:T(128)}, u32[]{:S(2)}) copy-start(s32[32]{0:T(128)} %param.11) | copy-start | bytes 388
  6.5 50.8 %all-gather.5.cloned.1.call-start = ((), (), s32[]{:S(2)}) async-start(), calls=%async_computation.3 | async-start | bytes 3342336 | tf_op jit(solution)/shard_map/all_gather | solution.py:200
  8.6 95.1 %all-gather.7.cloned.1.call-start = ((), (), s32[]{:S(2)}) async-start(), calls=%async_computation.4 | async-start | bytes 3342336 | tf_op jit(solution)/shard_map/all_gather | solution.py:200
  9.4 140.7 %all-gather.9.cloned.1.call-start = ((), (), s32[]{:S(2)}) async-start(), calls=%async_computation.5 | async-start | bytes 3342336 | tf_op jit(solution)/shard_map/all_gather | solution.py:200
  10.1 186.3 %all-gather.11.cloned.1.call-start = ((), (), s32[]{:S(2)}) async-start(), calls=%async_computation.6 | async-start | bytes 3342336 | tf_op jit(solution)/shard_map/all_gather | solution.py:200
  10.9 260.9 %reduce-scatter.2.cloned.1.call-start = ((), (), s32[]{:S(2)}) async-start(), calls=%async_computation.7 | async-start | bytes 4718592 | tf_op jit(solution)/shard_map/reduce_scatter | solution.py:210
  196.4 21.9 %copy-start.1 = (bf16[384,512]{1,0:T(8,128)(2,1)S(1)}, bf16[384,512]{1,0:T(8,128)(2,1)}, u32[]{:S(2)}) copy-start(bf16[384,512]{1,0:T(8,128)(2,1)} %attention.4) | copy-start | bytes 1179652
  196.4 21.9 %copy-start.2 = (bf16[384,512]{1,0:T(8,128)(2,1)S(1)}, bf16[384,512]{1,0:T(8,128)(2,1)}, u32[]{:S(2)}) copy-start(bf16[384,512]{1,0:T(8,128)(2,1)} %attention.5) | copy-start | bytes 1179652
  196.4 21.9 %copy-start.3 = (bf16[384,512]{1,0:T(8,128)(2,1)S(1)}, bf16[384,512]{1,0:T(8,128)(2,1)}, u32[]{:S(2)}) copy-start(bf16[384,512]{1,0:T(8,128)(2,1)} %attention.6) | copy-start | bytes 1179652
  275.2 29.3 %all-to-all-start = ((bf16[2,128,2048]{2,0,1:T(2,128)(2,1)}), bf16[2,128,2048]{2,0,1:T(2,128)(2,1)S(1)}, u32[]{:S(2)}, u32[]{:S(2)}) async-start(bf16[2,128,2048]{2,0,1:T(2,128)(2,1)} %copy.23), calls=%async_computation.1 | async-start | bytes 2097152 | tf_op jit(solution)/shard_map/all_to_all | solution.py:215
Sparse Core Ops, SparseCore 0:
  9.6 47.6 all-gather.4
  59.6 43.9 all-gather.6
  106.0 43.9 all-gather.8
  152.1 44.2 all-gather.10
  230.1 41.7 reduce-scatter.1
